TPU v7x, 512 devices: a whole 4x8x8 slice. The times are simulated.
512 devices in a mesh: pair: 128 (over z, y, core), blk: 4 (over x).
Axes of the slice: x: 4, y: 8, z: 8, core: 2. Of those that a mesh axis runs over, the one named last changes fastest.
Arguments:
- amplitudes: float32 [512, 16384], P('pair', 'blk'), may hold values from -6 to 6
- virt_ints: float32 [16384, 16384], P('blk', 'pair'), may hold values from -0.09375 to 0.09375
- virt_mask: int32 [128, 128], replicated, may hold values from 0 to 1, as said below
- hole_ints: float32 [512, 512], P('blk'), may hold values from -0.5 to 0.5
- hole_mask: int32 [4, 4], replicated, may hold values from 0 to 1, as said below
Outputs:
- residual: float32 [512, 16384], P('blk', 'pair')
Inputs may be any that keep to these rules, and one draw needn't show every extreme that they name: `virt_mask`: split the 128 block rows into four equal groups in order; in every block column, each group holds exactly 8 ones. `hole_mask`: every block column holds exactly one 1.
All inputs are finite; a program needn't handle non-finite values.
Results may differ from a plain program's by a relative error of at most 0.000057.
Values sent between devices are 32-bit elements; how exact they have to be, the bound alone decides.
No kernel may reach another device: no remote copies, remote signals or barrier semaphores. Data moves between devices by JAX's collectives and lax.ppermute only.
A program may use at most 64 MiB of HBM per device.

v0:
```python
import jax
import jax.numpy as jnp
from jax import lax
from jax.sharding import PartitionSpec as P

BS = 128
PRECISE = lax.Precision.HIGHEST


def block_pick(first, count, total_blocks):
    entry_ids = first + jnp.arange(count, dtype=jnp.int32)
    block_ids = jnp.arange(total_blocks, dtype=jnp.int32)
    return (entry_ids[:, None] // BS == block_ids[None, :]).astype(jnp.float32)


def local_mask(mask, row_first, row_count, col_first, col_count):
    total_blocks = mask.shape[0]
    rows_pick = block_pick(row_first, row_count, total_blocks)
    cols_pick = block_pick(col_first, col_count, total_blocks)
    inner = jnp.dot(mask.astype(jnp.float32), cols_pick.T, precision=PRECISE)
    return jnp.dot(rows_pick, inner, precision=PRECISE)


def per_device(amplitudes, virt_ints, virt_mask, hole_ints, hole_mask):
    pair_index = lax.axis_index("pair")
    blk_index = lax.axis_index("blk")
    pair_count = lax.axis_size("pair")
    local_rows, quarter = amplitudes.shape
    slab_width = virt_ints.shape[1]
    occupied = local_rows * pair_count
    virt_eff = virt_ints * local_mask(
        virt_mask, blk_index * quarter, quarter, pair_index * slab_width, slab_width
    )
    product = jnp.dot(
        lax.all_gather(amplitudes, "pair", axis=0, tiled=True), virt_eff, precision=PRECISE
    )
    particle = lax.psum_scatter(product, "blk", scatter_dimension=0, tiled=True)
    whole_rows = lax.all_gather(amplitudes, "blk", axis=1, tiled=True)
    owned = lax.all_to_all(whole_rows, "pair", split_axis=1, concat_axis=0, tiled=True)
    hole_rows = hole_ints.shape[0]
    hole_eff = hole_ints * local_mask(hole_mask, blk_index * hole_rows, hole_rows, 0, occupied)
    ladder = jnp.dot(hole_eff, owned, precision=PRECISE)
    return particle + ladder


def solution(mesh):
    placed = (P("pair", "blk"), P("blk", "pair"), P(), P("blk", None), P())
    return jax.shard_map(
        per_device, mesh=mesh, in_specs=placed, out_specs=P("blk", "pair"), check_vma=False
    )
```

profile of v0, /device:TPU:8, one launch (start us, length us, event | category | flops | bytes accessed | tf_op | source)
XLA Modules:
  0.0 159.2 jit_solution(10238636172915307327)
XLA Ops:
  6.5 0.0 all-gather.3.cloned.1.call-start
  6.5 0.7 all-gather.3.cloned.1.call-update
  7.3 14.2 %all_gather.7 = f32[4,16384]{1,0:T(4,128)} all-gather(f32[4,4096]{1,0:T(4,128)} %param.5), channel_id=1, replica_groups=mesh['pair'=128,'blk'=4] {'blk'}, dimensions={1}, use_global_device_ids=true | all-gather | bytes 327680 | tf_op jit(solution)/shard_map/all_gather | solution.py:38
  21.5 17.4 %all-to-all-start = ((f32[4,128,128]{2,0,1:T(4,128)}), f32[4,128,128]{2,0,1:T(4,128)S(1)}, u32[]{:S(2)}, u32[]{:S(2)}) async-start(f32[4,128,128]{2,0,1:T(4,128)} %bitcast.2), calls=%async_computation.1 | async-start | bytes 524288 | tf_op jit(solution)/shard_map/all_to_all | solution.py:39
  38.8 0.0 reduce-scatter.2.cloned.1.call-start
  38.9 1.1 fusion.3
  40.0 4.5 %convolution_multiply_fusion = f32[4096,128]{1,0:T(8,128)S(1)} fusion(f32[4096,128]{1,0:T(8,128)} %param.6, f32[128,128]{1,0:T(8,128)S(1)} %fusion.3, s32[4096]{0:T(1024)S(1)} %add_select_fusion), kind=kOutput, calls=%fused_computation | convolution fusion | flops 806354944 | bytes 4276224 | tf_op jit(solution)/shard_map/dot_general | solution.py:21
  44.5 60.8 %all-gather.3.cloned.1.call-done = f32[128,4,4096]{2,1,0:T(4,128)} async-done(((f32[1,4,4096]{2,1,0:T(4,128)}), f32[128,4,4096]{2,1,0:T(4,128)}) %all-gather.3.cloned.1.call-update) | async-done | bytes 8388624 | tf_op jit(solution)/shard_map/all_gather | solution.py:35
  105.4 10.0 %reshape.152 = f32[512,4096]{1,0:T(8,128)} reshape(f32[128,4,4096]{2,1,0:T(4,128)} %all-gather.3.cloned.1.call-done) | data formatting | bytes 16777216
  115.3 0.0 copy-start.1
  115.3 0.0 copy-start
  115.3 11.8 %convolution_bitcast_fusion = f32[512,128]{0,1:T(8,128)} fusion(f32[4096,128]{1,0:T(8,128)S(1)} %convolution_multiply_fusion, f32[512,4096]{1,0:T(8,128)} %reshape.152), kind=kOutput, calls=%fused_computation.2 | convolution fusion | flops 3221225472 | bytes 10747904 | tf_op jit(solution)/shard_map/dot_general | solution.py:34
  127.2 0.0 reduce-scatter.2.cloned.1.call-update
  127.2 0.0 copy-done.1
  127.2 0.3 fusion.1
  127.5 0.0 copy-done
  127.5 0.3 convolution_multiply_fusion.1
  127.9 0.0 all-to-all-done
  127.9 22.3 %reduce-scatter.2.cloned.1.call-done = f32[128,128]{0,1:T(8,128)} async-done(((f32[512,128]{0,1:T(8,128)}), f32[128,128]{0,1:T(8,128)}) %reduce-scatter.2.cloned.1.call-update) | async-done | bytes 65552 | tf_op jit(solution)/shard_map/reduce_scatter | solution.py:37
  150.2 1.4 convolution_add_fusion
  151.6 0.7 copy.13
  (4 shorter events, 0.0 us)
Async XLA Ops:
  6.5 98.8 %all-gather.3.cloned.1.call-start = ((), (), s32[]{:S(2)}) async-start(), calls=%async_computation.3 | async-start | bytes 8454144 | tf_op jit(solution)/shard_map/all_gather | solution.py:35
  21.5 106.4 %all-to-all-start = ((f32[4,128,128]{2,0,1:T(4,128)}), f32[4,128,128]{2,0,1:T(4,128)S(1)}, u32[]{:S(2)}, u32[]{:S(2)}) async-start(f32[4,128,128]{2,0,1:T(4,128)} %bitcast.2), calls=%async_computation.1 | async-start | bytes 524288 | tf_op jit(solution)/shard_map/all_to_all | solution.py:39
  38.8 111.3 %reduce-scatter.2.cloned.1.call-start = ((), (), s32[]{:S(2)}) async-start(), calls=%async_computation.2 | async-start | bytes 327680 | tf_op jit(solution)/shard_map/reduce_scatter | solution.py:37
  115.3 11.9 %copy-start.1 = (s32[4,4]{1,0:T(4,128)S(1)}, s32[4,4]{1,0:T(4,128)}, u32[]{:S(2)}) copy-start(s32[4,4]{1,0:T(4,128)} %param.9) | copy-start | bytes 196
  115.3 12.2 %copy-start = (f32[128,512]{1,0:T(8,128)S(1)}, f32[128,512]{1,0:T(8,128)}, u32[]{:S(2)}) copy-start(f32[128,512]{1,0:T(8,128)} %param.8) | copy-start | bytes 786436
Sparse Core Ops, SparseCore 0:
  10.5 94.8 all-gather.2
  127.3 22.8 reduce-scatter.1
where the time goes:
time: 160 us; the launch traced here: 159 us
  waiting for transfers between devices  83.9 us (52%)
  matrix products  19.4 us (12%)
  starting transfers between devices  17.4 us (11%)
  blocking collectives  14.2 us (9%)
  between operations  13.5 us (8%)
  local copies, waits for them, and re-layouts  10.7 us (7%)
    all_gather x1, waiting for transfers between devices, per_device(): lax.all_gather(amplitudes, 'pair', axis=0, tiled=True)  60.8 us
    reduce_scatter x1, waiting for transfers between devices, per_device(): particle = lax.psum_scatter(product, 'blk', scatter_dimension=0, tiled=True)  22.3 us
    all_to_all x1, starting transfers between devices, per_device(): lax.all_to_all(whole_rows, 'pair', split_axis=1, concat_axis=0, tiled=True)  17.4 us
    all_gather x1, blocking collectives, per_device(): whole_rows = lax.all_gather(amplitudes, 'blk', axis=1, tiled=True)  14.2 us
    dot_general x1, matrix products, per_device(): jnp.dot(lax.all_gather(amplitudes, 'pair', axis=0, tiled=True), virt_eff,...  11.8 us
    unnamed x5, local copies, waits for them, and re-layouts  9.99 us
    dot_general x2, matrix products, local_mask(): return jnp.dot(rows_pick, inner, precision=PRECISE)  4.78 us
  transfers between devices with their start and end apart: 3, of which 2 were waited for; matrix products, arithmetic and copies ran while one was open for 18% of the time, Pallas kernels for 0%

commit v1 on v0

--- a/solution.py
+++ b/solution.py
@@ -5,6 +5,18 @@
 
 BS = 128
 PRECISE = lax.Precision.HIGHEST
+
+
+def doubled_up(x, axis, dim):
+    ways, here = (lax.axis_size(axis), lax.axis_index(axis))
+    grown, reach = (x, 1)
+    while reach < ways:
+        theirs = lax.ppermute(grown, axis, [(d, d ^ reach) for d in range(ways)])
+        mine_first = jnp.concatenate([grown, theirs], axis=dim)
+        theirs_first = jnp.concatenate([theirs, grown], axis=dim)
+        grown = jnp.where(here & reach == 0, mine_first, theirs_first)
+        reach = 2 * reach
+    return grown
 
 
 def block_pick(first, count, total_blocks):
@@ -35,7 +47,7 @@
         lax.all_gather(amplitudes, "pair", axis=0, tiled=True), virt_eff, precision=PRECISE
     )
     particle = lax.psum_scatter(product, "blk", scatter_dimension=0, tiled=True)
-    whole_rows = lax.all_gather(amplitudes, "blk", axis=1, tiled=True)
+    whole_rows = doubled_up(amplitudes, "blk", 1)
     owned = lax.all_to_all(whole_rows, "pair", split_axis=1, concat_axis=0, tiled=True)
     hole_rows = hole_ints.shape[0]
     hole_eff = hole_ints * local_mask(hole_mask, blk_index * hole_rows, hole_rows, 0, occupied)

time: 160 us -> 160 us (level)
  blocking collectives: 14.2 us -> 0 us
  starting transfers between devices: 17.4 us -> 25.4 us
  waiting for transfers between devices: 83.9 us -> 89 us
    all_gather x1 -> x0, blocking collectives: 14.2 us -> none  [per_device(): whole_rows = lax.all_gather(amplitudes, 'blk', axis=1, tiled=True)]
    ppermute x0 -> x2, starting transfers between devices: none -> 8.04 us  [doubled_up(): theirs = lax.ppermute(grown, axis, [(d, d ^ reach) for d in range(ways)])]
    ppermute x0 -> x2, waiting for transfers between devices: none -> 3.66 us  [doubled_up(): theirs = lax.ppermute(grown, axis, [(d, d ^ reach) for d in range(ways)])]
    unnamed x5 -> x7, local copies, waits for them, and re-layouts: 9.99 us -> 10 us
  transfers between devices with their start and end apart: 3 -> 5, of which waited for: 2 -> 3; matrix products, arithmetic and copies ran while one was open for 18% -> 18% of each run, Pallas kernels for 0% -> 0%
where the time goes in v1:
time: 160 us; the launch traced here: 159 us
  waiting for transfers between devices  89 us (56%)
  starting transfers between devices  25.4 us (16%)
  matrix products  19.5 us (12%)
  between operations  13.6 us (8%)
  local copies, waits for them, and re-layouts  10.7 us (7%)
    all_gather x1, waiting for transfers between devices, per_device(): lax.all_gather(amplitudes, 'pair', axis=0, tiled=True)  62.3 us
    reduce_scatter x1, waiting for transfers between devices, per_device(): particle = lax.psum_scatter(product, 'blk', scatter_dimension=0, tiled=True)  22.3 us
    all_to_all x1, starting transfers between devices, per_device(): lax.all_to_all(whole_rows, 'pair', split_axis=1, concat_axis=0, tiled=True)  17.4 us
    dot_general x1, matrix products, per_device(): jnp.dot(lax.all_gather(amplitudes, 'pair', axis=0, tiled=True), virt_eff,...  11.8 us
    unnamed x7, local copies, waits for them, and re-layouts  10 us
    ppermute x2, starting transfers between devices, doubled_up(): theirs = lax.ppermute(grown, axis, [(d, d ^ reach) for d in range(ways)])  8.04 us
    dot_general x2, matrix products, local_mask(): return jnp.dot(rows_pick, inner, precision=PRECISE)  4.8 us
    ppermute x2, waiting for transfers between devices, doubled_up(): theirs = lax.ppermute(grown, axis, [(d, d ^ reach) for d in range(ways)])  3.66 us
  transfers between devices with their start and end apart: 5, of which 3 were waited for; matrix products, arithmetic and copies ran while one was open for 18% of the time, Pallas kernels for 0%

profile of v1, /device:TPU:8, one launch (start us, length us, event | category | flops | bytes accessed | tf_op | source)
XLA Modules:
  0.0 159.1 jit_solution(11916709904631685513)
XLA Ops:
  6.5 0.0 all-gather.3.cloned.1.call-start
  6.5 0.7 all-gather.3.cloned.1.call-update
  7.3 3.4 %collective-permute-start = (f32[4,4096]{1,0:T(4,128)}, f32[4,4096]{1,0:T(4,128)S(1)}, u32[]{:S(2)}, u32[]{:S(2)}) collective-permute-start(f32[4,4096]{1,0:T(4,128)} %param.5), channel_id=1, source_target_pairs={{0,1},{1,0},{2,3},{3,2},{4,5},{5,4},{6,7},{7,6},{8,9},{9,8},{10,11... | collective-permute-start | bytes 196616 | tf_op jit(solution)/shard_map/ppermute | solution.py:14
  10.7 1.1 fusion.3
  11.8 0.0 copy-start
  11.8 4.5 %convolution_multiply_fusion = f32[4096,128]{1,0:T(8,128)S(1)} fusion(f32[4096,128]{1,0:T(8,128)} %param.6, f32[128,128]{1,0:T(8,128)S(1)} %fusion.3, s32[4096]{0:T(1024)S(1)} %add_select_fusion), kind=kOutput, calls=%fused_computation | convolution fusion | flops 806354944 | bytes 4276224 | tf_op jit(solution)/shard_map/dot_general | solution.py:33
  16.3 0.0 collective-permute-done
  16.3 0.0 copy-done
  16.4 4.6 %collective-permute-start.1 = (f32[4,8192]{1,0:T(4,128)S(1)}, f32[4,8192]{1,0:T(4,128)S(1)}, u32[]{:S(2)}, u32[]{:S(2)}) collective-permute-start(f32[4,8192]{1,0:T(4,128)S(1)} %maximum_select_fusion.2), channel_id=1, source_target_pairs={{0,2},{1,3},{2,0},{3,1},{4,6},{5,7},{6,4},{7,5},{8,10},{9,11},{10,... | collective-permute-start | bytes 393224 | tf_op jit(solution)/shard_map/ppermute | solution.py:14
  21.1 3.7 %collective-permute-done.1 = f32[4,8192]{1,0:T(4,128)S(1)} collective-permute-done((f32[4,8192]{1,0:T(4,128)S(1)}, f32[4,8192]{1,0:T(4,128)S(1)}, u32[]{:S(2)}, u32[]{:S(2)}) %collective-permute-start.1) | collective-permute-done | bytes 131104 | tf_op jit(solution)/shard_map/ppermute | solution.py:14
  24.7 0.8 maximum_select_fusion
  25.5 17.4 %all-to-all-start = ((f32[4,128,128]{2,0,1:T(4,128)}), f32[4,128,128]{2,0,1:T(4,128)S(1)}, u32[]{:S(2)}, u32[]{:S(2)}) async-start(f32[4,128,128]{2,0,1:T(4,128)} %maximum_select_fusion), calls=%async_computation.1 | async-start | bytes 524288 | tf_op jit(solution)/shard_map/all_to_all | solution.py:51
  42.9 0.0 reduce-scatter.2.cloned.1.call-start
  42.9 62.3 %all-gather.3.cloned.1.call-done = f32[128,4,4096]{2,1,0:T(4,128)} async-done(((f32[1,4,4096]{2,1,0:T(4,128)}), f32[128,4,4096]{2,1,0:T(4,128)}) %all-gather.3.cloned.1.call-update) | async-done | bytes 8388624 | tf_op jit(solution)/shard_map/all_gather | solution.py:47
  105.3 10.0 %reshape.160 = f32[512,4096]{1,0:T(8,128)} reshape(f32[128,4,4096]{2,1,0:T(4,128)} %all-gather.3.cloned.1.call-done) | data formatting | bytes 16777216
  115.2 0.0 copy-start.2
  115.2 0.0 copy-start.1
  115.3 11.8 %convolution_bitcast_fusion = f32[512,128]{0,1:T(8,128)} fusion(f32[4096,128]{1,0:T(8,128)S(1)} %convolution_multiply_fusion, f32[512,4096]{1,0:T(8,128)} %reshape.160), kind=kOutput, calls=%fused_computation.2 | convolution fusion | flops 3221225472 | bytes 10747904 | tf_op jit(solution)/shard_map/dot_general | solution.py:46
  127.1 0.0 reduce-scatter.2.cloned.1.call-update
  127.1 0.0 copy-done.2
  127.1 0.3 fusion.1
  127.5 0.0 copy-done.1
  127.5 0.3 convolution_multiply_fusion.1
  127.8 0.0 all-to-all-done
  127.8 22.3 %reduce-scatter.2.cloned.1.call-done = f32[128,128]{0,1:T(8,128)} async-done(((f32[512,128]{0,1:T(8,128)}), f32[128,128]{0,1:T(8,128)}) %reduce-scatter.2.cloned.1.call-update) | async-done | bytes 65552 | tf_op jit(solution)/shard_map/reduce_scatter | solution.py:49
  150.1 1.4 convolution_add_fusion
  151.5 0.7 copy.23
  (6 shorter events, 0.1 us)
Async XLA Ops:
  6.5 98.7 %all-gather.3.cloned.1.call-start = ((), (), s32[]{:S(2)}) async-start(), calls=%async_computation.3 | async-start | bytes 8454144 | tf_op jit(solution)/shard_map/all_gather | solution.py:47
  7.3 9.1 %collective-permute-start = (f32[4,4096]{1,0:T(4,128)}, f32[4,4096]{1,0:T(4,128)S(1)}, u32[]{:S(2)}, u32[]{:S(2)}) collective-permute-start(f32[4,4096]{1,0:T(4,128)} %param.5), channel_id=1, source_target_pairs={{0,1},{1,0},{2,3},{3,2},{4,5},{5,4},{6,7},{7,6},{8,9},{9,8},{10,11... | collective-permute-start | bytes 196616 | tf_op jit(solution)/shard_map/ppermute | solution.py:14
  11.8 4.5 %copy-start = (f32[4,4096]{1,0:T(4,128)S(1)}, f32[4,4096]{1,0:T(4,128)}, u32[]{:S(2)}) copy-start(f32[4,4096]{1,0:T(4,128)} %param.5) | copy-start | bytes 196612
  16.4 8.4 %collective-permute-start.1 = (f32[4,8192]{1,0:T(4,128)S(1)}, f32[4,8192]{1,0:T(4,128)S(1)}, u32[]{:S(2)}, u32[]{:S(2)}) collective-permute-start(f32[4,8192]{1,0:T(4,128)S(1)} %maximum_select_fusion.2), channel_id=1, source_target_pairs={{0,2},{1,3},{2,0},{3,1},{4,6},{5,7},{6,4},{7,5},{8,10},{9,11},{10,... | collective-permute-start | bytes 393224 | tf_op jit(solution)/shard_map/ppermute | solution.py:14
  25.5 102.3 %all-to-all-start = ((f32[4,128,128]{2,0,1:T(4,128)}), f32[4,128,128]{2,0,1:T(4,128)S(1)}, u32[]{:S(2)}, u32[]{:S(2)}) async-start(f32[4,128,128]{2,0,1:T(4,128)} %maximum_select_fusion), calls=%async_computation.1 | async-start | bytes 524288 | tf_op jit(solution)/shard_map/all_to_all | solution.py:51
  42.9 107.2 %reduce-scatter.2.cloned.1.call-start = ((), (), s32[]{:S(2)}) async-start(), calls=%async_computation.2 | async-start | bytes 327680 | tf_op jit(solution)/shard_map/reduce_scatter | solution.py:49
  115.2 11.9 %copy-start.2 = (s32[4,4]{1,0:T(4,128)S(1)}, s32[4,4]{1,0:T(4,128)}, u32[]{:S(2)}) copy-start(s32[4,4]{1,0:T(4,128)} %param.9) | copy-start | bytes 196
  115.2 12.2 %copy-start.1 = (f32[128,512]{1,0:T(8,128)S(1)}, f32[128,512]{1,0:T(8,128)}, u32[]{:S(2)}) copy-start(f32[128,512]{1,0:T(8,128)} %param.8) | copy-start | bytes 786436
Sparse Core Ops, SparseCore 0:
  10.5 94.7 all-gather.2
  127.2 22.8 reduce-scatter.1
